TPU v7x, 128 devices: a whole 4x4x4 slice. The times are simulated.
128 devices in a mesh: frames: 32 (over z, x, core), rows: 4 (over y).
Axes of the slice: x: 4, y: 4, z: 4, core: 2. Of those that a mesh axis runs over, the one named last changes fastest.
Arguments:
- acts: bfloat16 [128, 12, 256, 256], P('frames', 'rows'), may hold values from -6 to 6
- grad_out: bfloat16 [128, 12, 256, 256], P('frames', 'rows'), may hold values from -6 to 6
- kernel: bfloat16 [3, 3, 3, 256, 256], replicated, may hold values from -0.078125 to 0.078125
Outputs:
- grad_acts: bfloat16 [128, 12, 256, 256], P('frames', 'rows')
- weight_grad: float32 [3, 3, 3, 256, 256], replicated
All inputs are finite; a program needn't handle non-finite values.
Results may differ from a plain program's by a relative error of at most 0.0031.
Values may be sent and summed in bfloat16 or wider, within the bound.
A program may use at most 256 MiB of HBM per device.

v0:
```python
import math

import jax
import jax.numpy as jnp
from jax import lax
from jax.sharding import PartitionSpec as P


def padded(cells, sides, width):
    for axis, dim in sides:
        count = lax.axis_size(axis)
        ends = count - 1
        head = lax.slice_in_dim(cells, 0, width, axis=dim)
        tail = lax.slice_in_dim(cells, cells.shape[dim] - width, cells.shape[dim], axis=dim)
        cells = jnp.concatenate(
            [
                lax.ppermute(tail, axis, [(i, (i + 1) % count) for i in range(ends)]),
                cells,
                lax.ppermute(head, axis, [((i + 1) % count, i) for i in range(ends)]),
            ],
            axis=dim,
        )
    return cells


def from_behind(value, axis, steps):
    count = lax.axis_size(axis)
    initial, last = (max(0, -steps), min(count, count - steps))
    return lax.ppermute(value, axis, [(source, source + steps) for source in range(initial, last)])


def on_device(acts, grad_out, kernel):
    frames_here = acts.shape[0]
    rows_here = acts.shape[1]
    width_here = acts.shape[3]
    x32 = acts.astype(jnp.float32)
    sig = jax.nn.sigmoid(x32)
    activ = (x32 * sig).astype(jnp.bfloat16)
    grad_rim = padded(grad_out, (("rows", 1),), 1)
    grad_next = from_behind(grad_rim[:2], "frames", -1)
    grad_ext = jnp.concatenate([grad_rim, grad_next], axis=0)
    grad_ext = jnp.pad(grad_ext, ((0, 0), (0, 0), (0, 0), (1, 1)))
    act_rim = padded(activ, (("rows", 1),), 1)
    act_prev = from_behind(act_rim[-2:], "frames", 1)
    act_ext = jnp.concatenate([act_prev, act_rim], axis=0)
    act_ext = jnp.pad(act_ext, ((0, 0), (0, 0), (0, 0), (1, 1)))
    grad_activ = jnp.zeros(x32.shape, jnp.float32)
    partial_terms = []
    for kt in range(3):
        for kh in range(3):
            for kw in range(3):
                piece = grad_ext[
                    2 - kt : 2 - kt + frames_here,
                    2 - kh : 2 - kh + rows_here,
                    :,
                    2 - kw : 2 - kw + width_here,
                ]
                grad_activ = grad_activ + jnp.einsum(
                    "thow,io->thiw", piece, kernel[kt, kh, kw], preferred_element_type=jnp.float32
                )
                shifted = act_ext[
                    kt : kt + frames_here, kh : kh + rows_here, :, kw : kw + width_here
                ]
                partial_terms.append(
                    jnp.einsum(
                        "thiw,thow->io", shifted, grad_out, preferred_element_type=jnp.float32
                    )
                )
    grad_acts = (grad_activ * sig * (1.0 + x32 * (1.0 - sig))).astype(jnp.bfloat16)
    local_sum = jnp.stack(partial_terms).reshape(3, 3, 3, kernel.shape[3], kernel.shape[4])
    total = lax.psum(local_sum, ("frames", "rows"))
    cells = frames_here * lax.axis_size("frames") * rows_here * lax.axis_size("rows") * width_here
    weight_grad = total * (1.0 / math.sqrt(cells))
    return (grad_acts, weight_grad)


def solution(mesh):
    placed = (P("frames", "rows", None, None), P("frames", "rows", None, None), P())
    return jax.shard_map(
        on_device,
        mesh=mesh,
        in_specs=placed,
        out_specs=(P("frames", "rows", None, None), P()),
        check_vma=False,
    )
```

profile of v0, /device:TPU:1, one launch (start us, length us, event | category | flops | bytes accessed | tf_op | source)
XLA Modules:
  0.0 329.8 jit_solution(5687872460502078687)
XLA Ops:
  10.0 4.8 %collective-permute-start = (bf16[4,1,256,256]{2,3,1,0:T(8,128)(2,1)}, bf16[4,1,256,256]{2,3,1,0:T(8,128)(2,1)}, u32[]{:S(2)}, u32[]{:S(2)}) collective-permute-start(bf16[4,1,256,256]{2,3,1,0:T(8,128)(2,1)} %get-tuple-element.33), channel_id=1, source_target_pairs={{0,1},{1,2},{2,3},{4,5},{5,6},{6,7},{8,9},{9,10},{10,11},{12,13},{... | collective-permute-start | bytes 1572872 | tf_op jit(solution)/shard_map/ppermute | solution.py:17
  20.4 4.6 %collective-permute-start.3 = (bf16[4,1,256,256]{2,3,1,0:T(8,128)(2,1)S(1)}, bf16[4,1,256,256]{2,3,1,0:T(8,128)(2,1)S(1)}, u32[]{:S(2)}, u32[]{:S(2)}) collective-permute-start(bf16[4,1,256,256]{2,3,1,0:T(8,128)(2,1)S(1)} %get-tuple-element.30), channel_id=1, source_target_pairs={{0,1},{1,2},{2,3},{4,5},{5,6},{6,7},{8,9},{9,10},{10,11},{12,13},{... | collective-permute-start | bytes 1572872 | tf_op jit(solution)/shard_map/ppermute | solution.py:17
  25.0 4.4 %collective-permute-done.1 = bf16[4,1,256,256]{2,3,1,0:T(8,128)(2,1)} collective-permute-done((bf16[4,1,256,256]{2,3,1,0:T(8,128)(2,1)}, bf16[4,1,256,256]{2,3,1,0:T(8,128)(2,1)}, u32[]{:S(2)}, u32[]{:S(2)}) %collective-permute-start.1) | collective-permute-done | bytes 524320 | tf_op jit(solution)/shard_map/ppermute | solution.py:19
  30.7 5.2 %collective-permute-start.2 = (bf16[2,5,256,256]{2,3,1,0:T(8,128)(2,1)S(1)}, bf16[2,5,256,256]{2,3,1,0:T(8,128)(2,1)S(1)}, u32[]{:S(2)}, u32[]{:S(2)}) collective-permute-start(bf16[2,5,256,256]{2,3,1,0:T(8,128)(2,1)S(1)} %pad_maximum_fusion.5), channel_id=1, source_target_pairs={{4,0},{8,4},{12,8},{16,12},{20,16},{24,20},{28,24},{32,28},{36,32}... | collective-permute-start | bytes 3932168 | tf_op jit(solution)/shard_map/ppermute | solution.py:29
  38.2 2.4 collective-permute-done.4
  40.8 5.2 %collective-permute-start.5 = (bf16[2,5,256,256]{2,3,1,0:T(8,128)(2,1)S(1)}, bf16[2,5,256,256]{2,3,1,0:T(8,128)(2,1)S(1)}, u32[]{:S(2)}, u32[]{:S(2)}) collective-permute-start(bf16[2,5,256,256]{2,3,1,0:T(8,128)(2,1)S(1)} %pad_maximum_fusion.3), channel_id=1, source_target_pairs={{0,4},{4,8},{8,12},{12,16},{16,20},{20,24},{24,28},{28,32},{32,36}... | collective-permute-start | bytes 3932168 | tf_op jit(solution)/shard_map/ppermute | solution.py:29
  48.0 3.3 %fusion.12 = f32[4,3,256,256]{3,2,1,0:T(8,128)} fusion(bf16[4,3,256,256]{2,3,1,0:T(8,128)(2,1)S(1)} %copy.5, bf16[4,1,256,256]{2,3,1,0:T(8,128)(2,1)} %collective-permute-done, bf16[3,3,3,256,256]{4,3,2,1,0:T(8,128)(2,1)S(1)} %copy-done.6), kind=kOutput, calls=%fused_computation.28 | convolution fusion | flops 406847488 | bytes 5373952 | tf_op jit(solution)/shard_map/thow,io->thiw/dot_general | solution.py:58
  51.3 3.3 %fusion.8 = f32[4,3,256,256]{3,2,1,0:T(8,128)} fusion(bf16[4,1,256,256]{2,3,1,0:T(8,128)(2,1)} %collective-permute-done.1, bf16[4,3,256,256]{2,3,1,0:T(8,128)(2,1)S(1)} %copy.5, bf16[3,3,3,256,256]{4,3,2,1,0:T(8,128)(2,1)S(1)} %copy-done.6), kind=kOutput, calls=%fused_computation.24 | convolution fusion | flops 406847488 | bytes 5373952 | tf_op jit(solution)/shard_map/thow,io->thiw/dot_general | solution.py:58
  56.6 2.7 fusion.71
  61.6 2.3 fusion.75
  63.9 2.4 fusion.77
  66.3 2.4 fusion.79
  73.2 2.3 fusion.85
  75.5 2.3 fusion.87
  84.5 2.3 fusion.95
  86.8 2.3 fusion.97
  91.9 2.3 fusion.375
  94.2 21.0 %pad_slice_fusion = (bf16[4,3,256,256]{2,3,1,0:T(8,128)(2,1)}, bf16[4,3,256,256]{2,3,1,0:T(8,128)(2,1)}, bf16[4,3,256,256]{2,3,1,0:T(8,128)(2,1)}, bf16[4,3,256,...) fusion(bf16[6,5,256,256]{2,3,1,0:T(8,128)(2,1)S(1)} %maximum_ma, ...), kind=kLoop, calls=%fused_computation.244 | loop fusion | bytes 21233664 | tf_op jit(solution)/shard_map/slice | solution.py:61
  115.3 8.4 %pad_slice_fusion.1 = (bf16[4,3,256,256]{2,3,1,0:T(8,128)(2,1)S(1)}, bf16[4,3,256,256]{2,3,1,0:T(8,128)(2,1)}, bf16[4,3,256,256]{2,3,1,0:T(8,128)(2,1)}, bf16[4,...) fusion(bf16[6,5,256,256]{2,3,1,0:T(8,128)(2,1)S(1)} %maximum_ma, ...), kind=kLoop, calls=%fused_computation.245 | loop fusion | bytes 25952256 | tf_op jit(solution)/shard_map/slice | solution.py:61
  153.0 3.0 copy-done.5
  157.3 3.4 %fusion.278 = f32[4,3,256,256]{3,2,1,0:T(8,128)} fusion(bf16[3,3,3,256,256]{4,3,2,1,0:T(8,128)(2,1)} %param.5, bf16[2,5,256,256]{2,3,1,0:T(8,128)(2,1)S(1)} %copy-done.31, bf16[4,1,256,256]{2,3,1,0:T(8,128)(2,1)} %collective-permute-done.1, bf16[4,3,256,256]{2,3,1,0:T(8,128)(2,1)S(1)} %copy.5, bf16[4,1,256,256]{2,3,1,0:T(8,128)(2,1)} %collective-permute-done), kind=kOutput, calls=%fused_computation.192 | convolution fusion | flops 418381824 | bytes 7208960 | tf_op jit(solution)/shard_map/thow,io->thiw/dot_general | solution.py:58
  160.7 3.3 fusion.282
  164.0 3.5 %fusion.286 = f32[4,3,256,256]{3,2,1,0:T(8,128)} fusion(bf16[3,3,3,256,256]{4,3,2,1,0:T(8,128)(2,1)} %param.5, bf16[2,5,256,256]{2,3,1,0:T(8,128)(2,1)S(1)} %copy-done.31, bf16[4,1,256,256]{2,3,1,0:T(8,128)(2,1)} %collective-permute-done.1, bf16[4,3,256,256]{2,3,1,0:T(8,128)(2,1)S(1)} %copy.5, bf16[4,1,256,256]{2,3,1,0:T(8,128)(2,1)} %collective-permute-done), kind=kOutput, calls=%fused_computation.200 | convolution fusion | flops 418381824 | bytes 7208960 | tf_op jit(solution)/shard_map/thow,io->thiw/dot_general | solution.py:58
  167.4 3.3 %fusion.290 = f32[4,3,256,256]{3,2,1,0:T(8,128)} fusion(bf16[3,3,3,256,256]{4,3,2,1,0:T(8,128)(2,1)} %param.5, bf16[2,5,256,256]{2,3,1,0:T(8,128)(2,1)S(1)} %copy-done.31, bf16[4,1,256,256]{2,3,1,0:T(8,128)(2,1)} %collective-permute-done.1, bf16[4,3,256,256]{2,3,1,0:T(8,128)(2,1)S(1)} %copy.5, bf16[4,1,256,256]{2,3,1,0:T(8,128)(2,1)} %collective-permute-done), kind=kOutput, calls=%fused_computation.204 | convolution fusion | flops 418381824 | bytes 7208960 | tf_op jit(solution)/shard_map/thow,io->thiw/dot_general | solution.py:58
  170.7 3.3 fusion.294
  174.0 3.4 %fusion.298 = f32[4,3,256,256]{3,2,1,0:T(8,128)} fusion(bf16[3,3,3,256,256]{4,3,2,1,0:T(8,128)(2,1)} %param.5, bf16[2,5,256,256]{2,3,1,0:T(8,128)(2,1)S(1)} %copy-done.31, bf16[4,1,256,256]{2,3,1,0:T(8,128)(2,1)} %collective-permute-done.1, bf16[4,3,256,256]{2,3,1,0:T(8,128)(2,1)S(1)} %copy.5, bf16[4,1,256,256]{2,3,1,0:T(8,128)(2,1)} %collective-permute-done), kind=kOutput, calls=%fused_computation.212 | convolution fusion | flops 418381824 | bytes 7208960 | tf_op jit(solution)/shard_map/thow,io->thiw/dot_general | solution.py:58
  177.4 3.2 fusion.101
  180.6 3.5 %fusion.103 = f32[4,3,256,256]{3,2,1,0:T(8,128)} fusion(bf16[3,3,3,256,256]{4,3,2,1,0:T(8,128)(2,1)} %param.5, bf16[6,5,256,256]{2,3,1,0:T(8,128)(2,1)S(1)} %copy-done.1), kind=kOutput, calls=%fused_computation.121 | convolution fusion | flops 402653184 | bytes 7208960 | tf_op jit(solution)/shard_map/thow,io->thiw/dot_general | solution.py:58
  184.1 28.4 %fusion.5 = bf16[4,3,256,256]{2,3,1,0:T(8,128)(2,1)} fusion(bf16[4,3,256,256]{2,3,1,0:T(8,128)(2,1)} %copy-done.4, f32[4,3,256,256]{3,2,1,0:T(8,128)} %fusion.12, f32[4,3,256,256]{3,2,1,0:T(8,128)} %fusion.71, f32[4,3,256,256]{3,2,1,0:T(8,128)} %fusion.73, f32[4,3,256,256]{3,2,1,0:T(8,128)S(1)} %copy-done.2, f32[4,3,256,256]{3,2,1,0:T(8,128)} %fusion.75, ...), kind=kOutput, calls=%fused_computation.11 | convolution fusion | flops 430964736 | bytes 88997888 | tf_op jit(solution)/shard_map/thow,io->thiw/dot_general | solution.py:58
  212.5 2.6 copy.66
  215.1 100.7 %all-reduce.4.cloned.1.call-done = f32[3,3,3,256,256]{4,3,2,1,0:T(8,128)} async-done(((f32[3,3,3,256,256]{4,3,2,1,0:T(8,128)}), f32[3,3,3,256,256]{4,3,2,1,0:T(8,128)}) %all-reduce.4.cloned.1.call-update) | async-done | bytes 7077904 | tf_op jit(solution)/shard_map/psum | solution.py:71
  315.8 6.9 %broadcast_multiply_fusion = f32[3,3,3,256,256]{4,3,2,1,0:T(8,128)} fusion(f32[3,3,3,256,256]{4,3,2,1,0:T(8,128)} %all-reduce.4.cloned.1.call-done), kind=kLoop, calls=%fused_computation.5 | loop fusion | flops 1769472 | bytes 14155776 | tf_op jit(solution)/shard_map/mul | solution.py:73
  (116 shorter events, 62.4 us)
Async XLA Ops:
  7.2 308.6 %all-reduce.4.cloned.1.call-start = ((), (), s32[]{:S(2)}) async-start(), calls=%async_computation | async-start | bytes 14155776 | tf_op jit(solution)/shard_map/psum | solution.py:71
  10.0 15.1 %collective-permute-start = (bf16[4,1,256,256]{2,3,1,0:T(8,128)(2,1)}, bf16[4,1,256,256]{2,3,1,0:T(8,128)(2,1)}, u32[]{:S(2)}, u32[]{:S(2)}) collective-permute-start(bf16[4,1,256,256]{2,3,1,0:T(8,128)(2,1)} %get-tuple-element.33), channel_id=1, source_target_pairs={{0,1},{1,2},{2,3},{4,5},{5,6},{6,7},{8,9},{9,10},{10,11},{12,13},{... | collective-permute-start | bytes 1572872 | tf_op jit(solution)/shard_map/ppermute | solution.py:17
  14.8 14.7 %collective-permute-start.1 = (bf16[4,1,256,256]{2,3,1,0:T(8,128)(2,1)}, bf16[4,1,256,256]{2,3,1,0:T(8,128)(2,1)}, u32[]{:S(2)}, u32[]{:S(2)}) collective-permute-start(bf16[4,1,256,256]{2,3,1,0:T(8,128)(2,1)} %get-tuple-element.32), channel_id=1, source_target_pairs={{1,0},{2,1},{3,2},{5,4},{6,5},{7,6},{9,8},{10,9},{11,10},{13,12},{... | collective-permute-start | bytes 1572872 | tf_op jit(solution)/shard_map/ppermute | solution.py:19
  17.8 130.5 %copy-start.4 = (bf16[4,3,256,256]{2,3,1,0:T(8,128)(2,1)}, bf16[4,3,256,256]{2,3,1,0:T(8,128)(2,1)S(1)}, u32[]{:S(2)}) copy-start(bf16[4,3,256,256]{2,3,1,0:T(8,128)(2,1)S(1)} %copy.11) | copy-start | bytes 4718596
  18.7 17.2 %copy-start.3 = (bf16[4,3,256,256]{3,2,1,0:T(8,128)(2,1)S(1)}, bf16[4,3,256,256]{3,2,1,0:T(8,128)(2,1)}, u32[]{:S(2)}) copy-start(bf16[4,3,256,256]{3,2,1,0:T(8,128)(2,1)} %param.4) | copy-start | bytes 4718596
  18.7 17.2 %copy-start.6 = (bf16[3,3,3,256,256]{4,3,2,1,0:T(8,128)(2,1)S(1)}, bf16[3,3,3,256,256]{4,3,2,1,0:T(8,128)(2,1)}, u32[]{:S(2)}) copy-start(bf16[3,3,3,256,256]{4,3,2,1,0:T(8,128)(2,1)} %param.5) | copy-start | bytes 10616836
  18.8 21.8 %collective-permute-start.4 = (bf16[4,1,256,256]{2,3,1,0:T(8,128)(2,1)S(1)}, bf16[4,1,256,256]{2,3,1,0:T(8,128)(2,1)S(1)}, u32[]{:S(2)}, u32[]{:S(2)}) collective-permute-start(bf16[4,1,256,256]{2,3,1,0:T(8,128)(2,1)S(1)} %get-tuple-element.31), channel_id=1, source_target_pairs={{1,0},{2,1},{3,2},{5,4},{6,5},{7,6},{9,8},{10,9},{11,10},{13,12},{... | collective-permute-start | bytes 1572872 | tf_op jit(solution)/shard_map/ppermute | solution.py:19
  20.4 20.2 %collective-permute-start.3 = (bf16[4,1,256,256]{2,3,1,0:T(8,128)(2,1)S(1)}, bf16[4,1,256,256]{2,3,1,0:T(8,128)(2,1)S(1)}, u32[]{:S(2)}, u32[]{:S(2)}) collective-permute-start(bf16[4,1,256,256]{2,3,1,0:T(8,128)(2,1)S(1)} %get-tuple-element.30), channel_id=1, source_target_pairs={{0,1},{1,2},{2,3},{4,5},{5,6},{6,7},{8,9},{9,10},{10,11},{12,13},{... | collective-permute-start | bytes 1572872 | tf_op jit(solution)/shard_map/ppermute | solution.py:17
  30.7 24.0 %collective-permute-start.2 = (bf16[2,5,256,256]{2,3,1,0:T(8,128)(2,1)S(1)}, bf16[2,5,256,256]{2,3,1,0:T(8,128)(2,1)S(1)}, u32[]{:S(2)}, u32[]{:S(2)}) collective-permute-start(bf16[2,5,256,256]{2,3,1,0:T(8,128)(2,1)S(1)} %pad_maximum_fusion.5), channel_id=1, source_target_pairs={{4,0},{8,4},{12,8},{16,12},{20,16},{24,20},{28,24},{32,28},{36,32}... | collective-permute-start | bytes 3932168 | tf_op jit(solution)/shard_map/ppermute | solution.py:29
  40.8 50.6 %collective-permute-start.5 = (bf16[2,5,256,256]{2,3,1,0:T(8,128)(2,1)S(1)}, bf16[2,5,256,256]{2,3,1,0:T(8,128)(2,1)S(1)}, u32[]{:S(2)}, u32[]{:S(2)}) collective-permute-start(bf16[2,5,256,256]{2,3,1,0:T(8,128)(2,1)S(1)} %pad_maximum_fusion.3), channel_id=1, source_target_pairs={{0,4},{4,8},{8,12},{12,16},{16,20},{20,24},{24,28},{28,32},{32,36}... | collective-permute-start | bytes 3932168 | tf_op jit(solution)/shard_map/ppermute | solution.py:29
  54.6 2.0 copy-start.30
  56.6 32.5 %copy-start = (bf16[6,5,256,256]{2,3,1,0:T(8,128)(2,1)}, bf16[6,5,256,256]{2,3,1,0:T(8,128)(2,1)S(1)}, u32[]{:S(2)}) copy-start(bf16[6,5,256,256]{2,3,1,0:T(8,128)(2,1)S(1)} %pad_maximum_fusion) | copy-start | bytes 11796484
  123.6 2.2 copy-start.19
  126.5 1.5 copy-start.28
  128.6 1.5 copy-start.27
  130.8 1.5 copy-start.15
  133.0 1.5 copy-start.24
  135.1 1.5 copy-start.23
  136.3 1.5 copy-start.22
  137.3 1.5 copy-start.13
  138.4 1.5 copy-start.12
  139.5 1.5 copy-start.11
  140.6 1.5 copy-start.21
  141.6 1.5 copy-start.10
  142.7 1.5 copy-start.9
  143.8 1.5 copy-start.17
  144.9 1.5 copy-start.8
  146.0 1.5 copy-start.7
  150.8 1.5 copy-start.20
  153.0 3.0 copy-start.5
  174.0 3.4 %copy-start.1 = (bf16[6,5,256,256]{2,3,1,0:T(8,128)(2,1)S(1)}, bf16[6,5,256,256]{2,3,1,0:T(8,128)(2,1)}, u32[]{:S(2)}) copy-start(bf16[6,5,256,256]{2,3,1,0:T(8,128)(2,1)} %copy-done) | copy-start | bytes 11796484
  180.6 3.5 %copy-start.2 = (f32[4,3,256,256]{3,2,1,0:T(8,128)S(1)}, f32[4,3,256,256]{3,2,1,0:T(8,128)}, u32[]{:S(2)}) copy-start(f32[4,3,256,256]{3,2,1,0:T(8,128)} %fusion.271) | copy-start | bytes 9437188
  (7 other events, 10.0 us)
Sparse Core Ops, SparseCore 0:
  156.1 159.6 all-reduce.3
where the time goes:
time: 334 us; the launch traced here: 330 us
  matrix products  118 us (35%)
  waiting for transfers between devices  108 us (32%)
  local copies, waits for them, and re-layouts  52.7 us (16%)
  starting transfers between devices  22.8 us (7%)
  between operations  14.9 us (4%)
  other arithmetic  13.6 us (4%)
    psum x1, waiting for transfers between devices, on_device(): total = lax.psum(local_sum, ('frames', 'rows'))  101 us
    dot_general x27, matrix products, on_device(): jnp.einsum('thow,io->thiw', piece, kernel[kt, kh, kw], preferred_element_...  98.8 us
    slice x3, local copies, waits for them, and re-layouts, on_device(): act_ext[kt:kt + frames_here, kh:kh + rows_here, :, kw:kw + width_here]  31.8 us
    unnamed x67, local copies, waits for them, and re-layouts  19.9 us
    dot_general x27, matrix products, on_device(): jnp.einsum('thiw,thow->io', shifted, grad_out, preferred_element_type=jnp...  19.4 us
    ppermute x2, starting transfers between devices, from_behind(): lax.ppermute(value, axis, [(source, source + steps) for source in range(i...  10.5 us
    ppermute x2, starting transfers between devices, padded(): lax.ppermute(tail, axis, [(i, (i + 1) % count) for i in range(ends)])  9.48 us
    mul x1, other arithmetic, on_device(): weight_grad = total * (1.0 / math.sqrt(cells))  6.92 us
  transfers between devices with their start and end apart: 7, of which 3 were waited for; matrix products, arithmetic and copies ran while one was open for 33% of the time, Pallas kernels for 0%

commit v1 on v0

v1 whole, which is shorter than its diff:
```python
import functools
import math

import jax
import jax.numpy as jnp
from jax import lax
from jax.experimental import pallas as pl
from jax.experimental.pallas import tpu as pltpu
from jax.sharding import PartitionSpec as P

MESH = pl.DeviceIdType.MESH
BF16, F32 = jnp.bfloat16, jnp.float32
AXES = "xyz"


def place():
    f = lax.axis_index("frames")
    return {"core": f % 2, "x": (f // 2) % 4, "z": f // 8, "y": lax.axis_index("rows")}


def device(at):
    return (at["z"] * 8 + at["x"] * 2 + at["core"], at["y"])


def moved(at, axis, steps):
    there = dict(at)
    size = 2 if axis == "core" else 4
    there[axis] = (at[axis] + steps + size) % size
    return device(there)


def body(
    acts_hbm, grad_hbm, kern_hbm, gacts_hbm, wsum_hbm,
    acts, g, k, a3, slope, w, cacc, gout, r0, s1, r1, s2, r2, s3, r3, w16,
    local_sem, halo_send, halo_recv, pair_send, pair_recv, ring_send, ring_recv,
):
    at = place()
    c = at["core"]
    f, r = lax.axis_index("frames"), lax.axis_index("rows")
    f_prev, f_next = (f + 31) % 32, (f + 1) % 32
    r_prev, r_next = (r + 3) % 4, (r + 1) % 4
    partner = moved(at, "core", 1)

    loads = [
        pltpu.make_async_copy(acts_hbm, acts, local_sem.at[0]),
        pltpu.make_async_copy(grad_hbm, g.at[pl.ds(0, 4), pl.ds(1, 3)], local_sem.at[1]),
        pltpu.make_async_copy(kern_hbm, k, local_sem.at[2]),
    ]
    for load in loads:
        load.start()

    barrier = pltpu.get_barrier_semaphore()
    peers = [partner, (f_prev, r), (f_next, r)]
    peers += [moved(at, axis, d) for axis in AXES for d in (1, 2, 3)]
    for peer in peers:
        pl.semaphore_signal(barrier, inc=1, device_id=peer, device_id_type=MESH)
    pl.semaphore_wait(barrier, len(peers))

    def remote(src, dst, ssem, rsem, to):
        return pltpu.make_async_remote_copy(
            src_ref=src, dst_ref=dst, send_sem=ssem, recv_sem=rsem,
            device_id=to, device_id_type=MESH,
        )

    def halo(n, src, dst, to):
        return remote(src, dst, halo_send.at[n], halo_recv.at[n], to)

    early, late, beyond = pl.ds(0, 2), pl.ds(2, 2), pl.ds(4, 2)
    halos = [
        halo(0, grad_hbm.at[early, 2], g.at[early, 0], (f, r_next)),
        halo(1, grad_hbm.at[early, 0], g.at[early, 4], (f, r_prev)),
        halo(2, grad_hbm.at[early], g.at[beyond, pl.ds(1, 3)], (f_prev, r)),
        halo(3, grad_hbm.at[late, 2], g.at[late, 0], (f, r_next)),
        halo(4, grad_hbm.at[late, 0], g.at[late, 4], (f, r_prev)),
        halo(5, g.at[early, 0], g.at[beyond, 0], (f_prev, r)),
        halo(6, g.at[early, 4], g.at[beyond, 4], (f_prev, r)),
    ]
    for copy in halos[:5]:
        copy.start()

    loads[0].wait()
    lane = lax.broadcasted_iota(jnp.int32, (256, 256), 1)

    @pl.loop(0, 12)
    def _(n):
        t, h = n // 3, n % 3
        x = acts[t, h].astype(F32)
        sig = jax.nn.sigmoid(x)
        activ = (x * sig).astype(BF16)
        slope[t, h] = sig * (1.0 + x * (1.0 - sig))
        wide = activ.astype(F32)
        a3[t, h, 1] = activ
        a3[t, h, 0] = jnp.where(lane == 0, 0.0, pltpu.roll(wide, 1, 1)).astype(BF16)
        a3[t, h, 2] = jnp.where(lane == 255, 0.0, pltpu.roll(wide, 255, 1)).astype(BF16)

    def weight_part(kt, kh, t, hs, write=False):
        acc = None if write else w[kt * 3 + kh].reshape(768, 256)
        for h in hs:
            term = lax.dot_general(
                a3[t, h].reshape(768, 256), g[t + 2 - kt, h + 2 - kh],
                (((1,), (1,)), ((), ())), preferred_element_type=F32,
            )
            acc = term if acc is None else acc + term
        w[kt * 3 + kh] = acc.reshape(3, 256, 256)

    def input_part(kt, t, h, khs, write=False):
        acc = None if write else cacc[t, h]
        for kh in khs:
            term = jnp.dot(
                k[kt, kh].reshape(768, 256), g[t + 2 - kt, h + 2 - kh],
                preferred_element_type=F32,
            )
            acc = term if acc is None else acc + term
        cacc[t, h] = acc

    inner_h = {0: (0, 1), 1: (0, 1, 2), 2: (1, 2)}
    inner_kh = {0: (0, 1), 1: (0, 1, 2), 2: (1, 2)}

    loads[1].wait()

    @pl.loop(0, 3)
    def _(kt):
        for kh in range(3):
            weight_part(kt, kh, 0, inner_h[kh], write=True)

        @pl.loop(1, kt + 2)
        def _(t):
            for kh in range(3):
                weight_part(kt, kh, t, inner_h[kh])

    loads[2].wait()

    @pl.loop(0, 4)
    def _(t):
        for h in range(3):
            input_part(2, t, h, inner_kh[h], write=True)

        @pl.loop(jnp.maximum(t - 1, 0), 2)
        def _(kt):
            for h in range(3):
                input_part(kt, t, h, inner_kh[h])

    def clear(frames, row):
        for t in frames:
            g[t, row] = jnp.zeros((256, 256), BF16)

    def edge_rows(frames):
        @pl.when(r == 0)
        def _():
            clear(frames, 0)

        @pl.when(r == 3)
        def _():
            clear(frames, 4)

    halos[0].wait_recv()
    halos[1].wait_recv()
    edge_rows((0, 1))
    halos[5].start()
    halos[6].start()
    halos[3].wait_recv()
    halos[4].wait_recv()
    edge_rows((2, 3))

    def pair_sum(kt):
        return remote(
            w.at[pl.ds(3 * kt, 3), :, pl.ds(pl.multiple_of(128 * (1 - c), 128), 128)],
            r0.at[kt], pair_send.at[kt], pair_recv.at[kt], partner,
        )

    def pair_gather(kt, half):
        part = w16.at[pl.ds(3 * kt, 3), :, pl.ds(pl.multiple_of(128 * half, 128), 128)]
        return remote(part, part, pair_send.at[3 + kt], pair_recv.at[3 + kt], partner)

    def ring(stage, kt, kw, d, src, dst, axis):
        n = ((stage * 3 + kt) * 3 + kw) * 3 + d
        return remote(src, dst, ring_send.at[n], ring_recv.at[n], moved(at, axis, d + 1))

    def order(kw):
        return AXES[kw], AXES[(kw + 1) % 3], AXES[(kw + 2) % 3]

    def tile(p):
        return (
            pl.ds(pl.multiple_of(16 * (p // 2), 16), 16),
            pl.ds(pl.multiple_of(128 * (p % 2), 128), 128),
        )

    def rows32(p):
        return pl.ds(pl.multiple_of(32 * p, 32), 32)

    def scatter_one(kt, kw, d):
        first = order(kw)[0]
        to = (at[first] + d + 1) % 4
        return ring(0, kt, kw, d, s1.at[kt, kw, :, rows32(to)], r1.at[kt, kw, d], first)

    def scatter_two(kt, kw, d):
        second = order(kw)[1]
        rows, cols = tile((at[second] + d + 1) % 4)
        return ring(1, kt, kw, d, s2.at[kt, kw, :, rows, cols], r2.at[kt, kw, d], second)

    def sum_three(kt, kw, d):
        return ring(2, kt, kw, d, s3.at[kt, kw], r3.at[kt, kw, d], order(kw)[2])

    def gather_two(kt, kw, d, back=0):
        first, second, _ = order(kw)
        rows, cols = tile((at[second] + 4 - back) % 4)
        rows = pl.ds(
            pl.multiple_of(128 * c + 32 * at[first] + 16 * (((at[second] + 4 - back) % 4) // 2), 16), 16
        )
        part = w16.at[pl.ds(3 * kt, 3), kw, rows, cols]
        return ring(3, kt, kw, d, part, part, second)

    def gather_one(kt, kw, d, back=0):
        first = order(kw)[0]
        part = w16.at[
            pl.ds(3 * kt, 3), kw,
            pl.ds(pl.multiple_of(128 * c + 32 * ((at[first] + 4 - back) % 4), 32), 32),
        ]
        return ring(4, kt, kw, d, part, part, first)

    def start_pair(kt):
        pair_sum(kt).start()

    def start_one(kt):
        pair_sum(kt).wait_recv()
        mine = pl.ds(pl.multiple_of(128 * c, 128), 128)
        for kw in range(3):
            for kh in range(3):
                s1[kt, kw, kh] = (w[3 * kt + kh, kw, mine] + r0[kt, kh, kw]).astype(BF16)
            for d in range(3):
                scatter_one(kt, kw, d).start()

    def start_two(kt):
        for kw in range(3):
            p = at[order(kw)[0]]
            for d in range(3):
                scatter_one(kt, kw, d).wait_recv()
            own = pl.ds(pl.multiple_of(128 * c + 32 * p, 32), 32)
            for kh in range(3):
                total = w[3 * kt + kh, kw, own] + r0[kt, kh, kw, rows32(p)]
                for d in range(3):
                    total = total + r1[kt, kw, d, kh].astype(F32)
                s2[kt, kw, kh] = total
            for d in range(3):
                scatter_two(kt, kw, d).start()

    def start_three(kt):
        for kw in range(3):
            rows, cols = tile(at[order(kw)[1]])
            for d in range(3):
                scatter_two(kt, kw, d).wait_recv()
            total = s2[kt, kw, :, rows, cols]
            for d in range(3):
                total = total + r2[kt, kw, d]
            s3[kt, kw] = total
            for d in range(3):
                sum_three(kt, kw, d).start()

    def start_gather_two(kt):
        for kw in range(3):
            first, second, _ = order(kw)
            rows, cols = tile(at[second])
            for d in range(3):
                sum_three(kt, kw, d).wait_recv()
            total = (s3[kt, kw] + r3[kt, kw, 1]) + (r3[kt, kw, 0] + r3[kt, kw, 2])
            rows = pl.ds(pl.multiple_of(128 * c + 32 * at[first] + 16 * (at[second] // 2), 16), 16)
            w16[pl.ds(3 * kt, 3), kw, rows, cols] = total.astype(BF16)
            for d in range(3):
                gather_two(kt, kw, d).start()

    def start_gather_one(kt):
        for kw in range(3):
            for d in range(3):
                gather_two(kt, kw, d, d + 1).wait_recv()
            for d in range(3):
                gather_one(kt, kw, d).start()

    def start_pair_gather(kt):
        for kw in range(3):
            for d in range(3):
                gather_one(kt, kw, d, d + 1).wait_recv()
        pair_gather(kt, c).start()

    def write_out(kt):
        part = pl.ds(3 * kt, 3)
        return pltpu.make_async_copy(w16.at[part], wsum_hbm.at[part], local_sem.at[4 + kt])

    def finish(kt):
        pair_gather(kt, 1 - c).wait_recv()
        write_out(kt).start()

    def edge_weights(kt):
        @pl.loop(0, kt + 2)
        def _(t):
            weight_part(kt, 0, t, (2,))
            weight_part(kt, 2, t, (0,))

    edge_weights(2)
    start_pair(2)
    edge_weights(1)
    start_one(2)
    edge_weights(0)

    halos[2].wait_recv()
    halos[5].wait_recv()
    halos[6].wait_recv()

    @pl.when(f == 31)
    def _():
        for row in range(5):
            clear((4, 5), row)

    for kh in range(3):
        weight_part(1, kh, 3, (0, 1, 2))
    start_pair(1)
    start_two(2)

    @pl.loop(2, 4)
    def _(t):
        for kh in range(3):
            weight_part(0, kh, t, (0, 1, 2))

    start_pair(0)
    start_one(1)
    start_three(2)

    def finish_input(t):
        for h in range(3):
            y = cacc[t, h]
            left = jnp.where(lane == 255, 0.0, pltpu.roll(y[:256], 255, 1))
            right = jnp.where(lane == 0, 0.0, pltpu.roll(y[512:], 1, 1))
            gout[t, h] = ((y[256:512] + left + right) * slope[t, h]).astype(BF16)

    def edge_inputs(t):
        @pl.loop(max(t - 1, 0), 3)
        def _(kt):
            input_part(kt, t, 0, (2,))
            input_part(kt, t, 2, (0,))

        @pl.loop(0, max(t - 1, 0))
        def _(kt):
            for h in range(3):
                input_part(kt, t, h, (0, 1, 2))

        finish_input(t)

    edge_inputs(0)
    start_one(0)
    start_two(1)
    start_gather_two(2)
    edge_inputs(1)
    start_two(0)
    start_three(1)
    start_gather_one(2)
    edge_inputs(2)
    start_three(0)
    start_gather_two(1)
    start_pair_gather(2)
    edge_inputs(3)
    result = pltpu.make_async_copy(gout, gacts_hbm, local_sem.at[3])
    result.start()
    start_gather_two(0)
    start_gather_one(1)
    finish(2)
    start_gather_one(0)
    start_pair_gather(1)
    start_pair_gather(0)
    finish(1)
    finish(0)

    result.wait()
    for copy in halos:
        copy.wait_send()
    for kt in range(3):
        write_out(kt).wait()
        pair_sum(kt).wait_send()
        pair_gather(kt, c).wait_send()
        for kw in range(3):
            for d in range(3):
                for step in (scatter_one, scatter_two, sum_three, gather_two, gather_one):
                    step(kt, kw, d).wait_send()


def fused(acts, grad_out, kernel):
    flops = 4 * 27 * 256 * 256 * 3072
    dma = pltpu.SemaphoreType.DMA
    return pl.pallas_call(
        body,
        out_shape=(
            jax.ShapeDtypeStruct(acts.shape, BF16),
            jax.ShapeDtypeStruct((9, 3, 256, 256), BF16),
        ),
        in_specs=[pl.BlockSpec(memory_space=pl.ANY)] * 3,
        out_specs=(pl.BlockSpec(memory_space=pl.ANY),) * 2,
        scratch_shapes=[
            pltpu.VMEM((4, 3, 256, 256), BF16),
            pltpu.VMEM((6, 5, 256, 256), BF16),
            pltpu.VMEM((3, 3, 3, 256, 256), BF16),
            pltpu.VMEM((4, 3, 3, 256, 256), BF16),
            pltpu.VMEM((4, 3, 256, 256), F32),
            pltpu.VMEM((9, 3, 256, 256), F32),
            pltpu.VMEM((4, 3, 768, 256), F32),
            pltpu.VMEM((4, 3, 256, 256), BF16),
            pltpu.VMEM((3, 3, 3, 128, 256), F32),
            pltpu.VMEM((3, 3, 3, 128, 256), BF16),
            pltpu.VMEM((3, 3, 3, 3, 32, 256), BF16),
            pltpu.VMEM((3, 3, 3, 32, 256), F32),
            pltpu.VMEM((3, 3, 3, 3, 16, 128), F32),
            pltpu.VMEM((3, 3, 3, 16, 128), F32),
            pltpu.VMEM((3, 3, 3, 3, 16, 128), F32),
            pltpu.VMEM((9, 3, 256, 256), BF16),
            dma((7,)),
            dma((7,)),
            dma((7,)),
            dma((6,)),
            dma((6,)),
            dma((135,)),
            dma((135,)),
        ],
        compiler_params=pltpu.CompilerParams(
            collective_id=0, has_side_effects=True, vmem_limit_bytes=60 * 2**20
        ),
        cost_estimate=pl.CostEstimate(flops=flops, bytes_accessed=16_000_000, transcendentals=0),
        name="conv_grads",
    )(acts, grad_out, kernel)


def on_device(acts, grad_out, kernel):
    cells = 1
    for dim, axis in ((0, "frames"), (1, "rows")):
        cells *= acts.shape[dim] * lax.axis_size(axis)
    cells *= acts.shape[3]
    grad_acts, total = fused(acts, grad_out, kernel)
    weight_grad = total.astype(F32).reshape(kernel.shape) * (1.0 / math.sqrt(cells))
    return (grad_acts, weight_grad)


def solution(mesh):
    placed = (P("frames", "rows", None, None), P("frames", "rows", None, None), P())
    return jax.shard_map(
        on_device,
        mesh=mesh,
        in_specs=placed,
        out_specs=(P("frames", "rows", None, None), P()),
        check_vma=False,
    )
```

time: 334 us -> 82.4 us (0.25); the launches traced: 330 us -> 82.3 us
  matrix products: 118 us -> 0 us
  waiting for transfers between devices: 108 us -> 0 us
  Pallas kernels: 0 us -> 74.5 us
  local copies, waits for them, and re-layouts: 52.7 us -> 1.15 us
  starting transfers between devices: 22.8 us -> 0 us
  between operations: 14.9 us -> 0.65 us
  other arithmetic: 13.6 us -> 5.97 us
    dot_general x54 -> x0, matrix products: 118 us -> none  [the longest x27 98.8 us: on_device(): jnp.einsum('thow,io->thiw', piece, kernel[kt, kh, kw], preferred_element_...]
    psum x1 -> x0, waiting for transfers between devices: 101 us -> none  [on_device(): total = lax.psum(local_sum, ('frames', 'rows'))]
    pallas_call x0 -> x1, Pallas kernels: none -> 74.5 us  [fused(): pl.pallas_call(body, out_shape=(jax.ShapeDtypeStruct(acts.shape, BF16), j...]
    slice x5 -> x0, local copies, waits for them, and re-layouts: 32.9 us -> none  [the longest x3 31.8 us: on_device(): act_ext[kt:kt + frames_here, kh:kh + rows_here, :, kw:kw + width_here]]
    ppermute x6 -> x0, starting transfers between devices: 22.8 us -> none  [the longest x2 10.5 us: from_behind(): lax.ppermute(value, axis, [(source, source + steps) for source in range(i...]
    unnamed x67 -> x3, local copies, waits for them, and re-layouts: 19.9 us -> 1.15 us
    ppermute x6 -> x0, waiting for transfers between devices: 6.86 us -> none  [the longest x2 6.85 us: padded(): lax.ppermute(head, axis, [((i + 1) % count, i) for i in range(ends)])]
    concatenate x5 -> x0, other arithmetic: 5.76 us -> none  [the longest x3 3.29 us: padded(): jnp.concatenate([lax.ppermute(tail, axis, [(i, (i + 1) % count) for i in...]
  transfers between devices with their start and end apart: 7 -> 0, of which waited for: 3 -> 0; matrix products, arithmetic and copies ran while one was open for 33% -> 0% of each run, Pallas kernels for 0% -> 0%
where the time goes in v1:
time: 82.4 us; the launch traced here: 82.3 us
  Pallas kernels  74.5 us (90%)
  other arithmetic  5.97 us (7%)
  local copies, waits for them, and re-layouts  1.15 us (1%)
    pallas_call x1, Pallas kernels, fused(): pl.pallas_call(body, out_shape=(jax.ShapeDtypeStruct(acts.shape, BF16), j...  74.5 us
    mul x1, other arithmetic, on_device(): total.astype(F32).reshape(kernel.shape) * (1.0 / math.sqrt(cells))  5.97 us

profile of v1, /device:TPU:1, one launch (start us, length us, event | category | flops | bytes accessed | tf_op | source)
XLA Modules:
  0.0 82.3 jit_solution(15892153586967659939)
XLA Ops:
  0.6 74.5 %conv_grads.1 = (bf16[4,3,256,256]{3,2,1,0:T(8,128)(2,1)}, bf16[9,3,256,256]{3,2,1,0:T(8,128)(2,1)}) custom-call(bf16[4,3,256,256]{3,2,1,0:T(8,128)(2,1)} %acts_hbm.1, bf16[4,3,256,256]{3,2,1,0:T(8,128)(2,1)} %grad_hbm.1, bf16[3,3,3,256,256]{4,3,2,1,0:T(8,128)(2,1)} %kern_hbm.1), custom_call_target="tpu_custom_call" | custom-call | flops 21743271936 | bytes 16000000 | tf_op jit(solution)/shard_map/conv_grads/pallas_call | solution.py:387
  75.2 0.0 copy-start
  75.2 6.0 %convert_multiply_fusion = f32[9,3,256,256]{3,2,1,0:T(8,128)} fusion(bf16[9,3,256,256]{3,2,1,0:T(8,128)(2,1)} %get-tuple-element.5), kind=kLoop, calls=%fused_computation | loop fusion | flops 3538944 | bytes 10616832 | tf_op jit(solution)/shard_map/mul | solution.py:434
  81.1 0.0 copy-done
  81.1 1.1 %copy.6 = bf16[4,3,256,256]{3,2,1,0:T(8,128)(2,1)} copy(bf16[4,3,256,256]{3,2,1,0:T(8,128)(2,1)S(1)} %copy-done) | data formatting | bytes 3145728
Async XLA Ops:
  75.2 6.0 %copy-start = (bf16[4,3,256,256]{3,2,1,0:T(8,128)(2,1)S(1)}, bf16[4,3,256,256]{3,2,1,0:T(8,128)(2,1)}, u32[]{:S(2)}) copy-start(bf16[4,3,256,256]{3,2,1,0:T(8,128)(2,1)} %get-tuple-element.8) | copy-start | bytes 4718596

commit v2 on v0

v2 whole, which is shorter than its diff:
```python
import functools
import math

import jax
import jax.numpy as jnp
from jax import lax
from jax.experimental import pallas as pl
from jax.experimental.pallas import tpu as pltpu
from jax.sharding import PartitionSpec as P

MESH = pl.DeviceIdType.MESH
BF16, F32 = jnp.bfloat16, jnp.float32
AXES = "xyz"
TAPS = ((2, 1), (1, 1), (0, 1), (2, 0), (2, 2), (1, 0), (1, 2), (0, 0), (0, 2))
BATCHES = ((0, 3), (3, 2), (5, 2), (7, 2))


def place():
    f = lax.axis_index("frames")
    return {"core": f % 2, "x": (f // 2) % 4, "z": f // 8, "y": lax.axis_index("rows")}


def device(at):
    return (at["z"] * 8 + at["x"] * 2 + at["core"], at["y"])


def moved(at, axis, steps):
    there = dict(at)
    size = 2 if axis == "core" else 4
    there[axis] = (at[axis] + steps + size) % size
    return device(there)


def body(
    acts_hbm, grad_hbm, kern_hbm, gout, w16,
    acts, g, gt, k, a3, slope, w, r0, s1, r1, s2, r2, s3, r3,
    local_sem, halo_send, halo_recv, pair_send, pair_recv, ring_send, ring_recv,
):
    at = place()
    c = at["core"]
    f, r = lax.axis_index("frames"), lax.axis_index("rows")
    f_prev, f_next = (f + 31) % 32, (f + 1) % 32
    r_prev, r_next = (r + 3) % 4, (r + 1) % 4
    partner = moved(at, "core", 1)

    loads = [
        pltpu.make_async_copy(acts_hbm, acts, local_sem.at[0]),
        pltpu.make_async_copy(grad_hbm, g.at[pl.ds(0, 4), pl.ds(1, 3)], local_sem.at[1]),
        pltpu.make_async_copy(kern_hbm, k, local_sem.at[2]),
    ]
    for load in loads:
        load.start()

    barrier = pltpu.get_barrier_semaphore()
    peers = [partner, (f_prev, r), (f_next, r)]
    peers += [moved(at, axis, d) for axis in AXES for d in (1, 2, 3)]
    for peer in peers:
        pl.semaphore_signal(barrier, inc=1, device_id=peer, device_id_type=MESH)
    pl.semaphore_wait(barrier, len(peers))

    def remote(src, dst, ssem, rsem, to):
        return pltpu.make_async_remote_copy(
            src_ref=src, dst_ref=dst, send_sem=ssem, recv_sem=rsem,
            device_id=to, device_id_type=MESH,
        )

    def halo(n, src, dst, to):
        return remote(src, dst, halo_send.at[n], halo_recv.at[n], to)

    early, late, beyond = pl.ds(0, 2), pl.ds(2, 2), pl.ds(4, 2)
    halos = [
        halo(0, grad_hbm.at[early, 2], g.at[early, 0], (f, r_next)),
        halo(1, grad_hbm.at[early, 0], g.at[early, 4], (f, r_prev)),
        halo(2, grad_hbm.at[early], g.at[beyond, pl.ds(1, 3)], (f_prev, r)),
        halo(3, grad_hbm.at[late, 2], g.at[late, 0], (f, r_next)),
        halo(4, grad_hbm.at[late, 0], g.at[late, 4], (f, r_prev)),
        halo(5, g.at[early, 0], g.at[beyond, 0], (f_prev, r)),
        halo(6, g.at[early, 4], g.at[beyond, 4], (f_prev, r)),
    ]
    for copy in halos[:3]:
        copy.start()

    lane = lax.broadcasted_iota(jnp.int32, (256, 256), 1)

    def activate(t, h):
        x = acts[t, h].astype(F32)
        sig = jax.nn.sigmoid(x)
        activ = (x * sig).astype(BF16)
        slope[t, h] = sig * (1.0 + x * (1.0 - sig))
        wide = activ.astype(F32)
        a3[t, h, 1] = activ
        a3[t, h, 0] = jnp.where(lane == 0, 0.0, pltpu.roll(wide, 1, 1)).astype(BF16)
        a3[t, h, 2] = jnp.where(lane == 255, 0.0, pltpu.roll(wide, 255, 1)).astype(BF16)

    def turn(t, row):
        gt[t, row] = g[t, row].T

    HERE, ABOVE_BELOW, NEXT = range(3)

    def weight_part(n, parts, more=False):
        kt, kh = TAPS[n]
        acc = w[n].reshape(768, 256) if more else None
        for t in range(4):
            for h in range(3):
                frame, row = t + 2 - kt, h + 2 - kh
                part = NEXT if frame > 3 else HERE if 1 <= row <= 3 else ABOVE_BELOW
                if part not in parts:
                    continue
                term = jnp.dot(
                    a3[t, h].reshape(768, 256), gt[frame, row], preferred_element_type=F32
                )
                acc = term if acc is None else acc + term
        w[n] = acc.reshape(3, 256, 256)

    def input_grad(t, h):
        y = None
        for kt in range(3):
            for kh in range(3):
                term = jnp.dot(
                    k[kt, kh].reshape(768, 256), g[t + 2 - kt, h + 2 - kh],
                    preferred_element_type=F32,
                )
                y = term if y is None else y + term
        left = jnp.where(lane == 255, 0.0, pltpu.roll(y[:256], 255, 1))
        right = jnp.where(lane == 0, 0.0, pltpu.roll(y[512:], 1, 1))
        gout[t, h] = ((y[256:512] + left + right) * slope[t, h]).astype(BF16)

    loads[0].wait()
    loads[1].wait()

    @pl.loop(0, 4)
    def _(t):
        for h in range(3):
            activate(t, h)
            turn(t, h + 1)

    def clear(frames, row):
        for t in frames:
            g[t, row] = jnp.zeros((256, 256), BF16)

    def edge_rows(frames):
        @pl.when(r == 0)
        def _():
            clear(frames, 0)

        @pl.when(r == 3)
        def _():
            clear(frames, 4)

    def taps(batch):
        return pl.ds(*BATCHES[batch])

    def pair_sum(batch):
        return remote(
            w.at[taps(batch), :, pl.ds(pl.multiple_of(128 * (1 - c), 128), 128)],
            r0.at[taps(batch)], pair_send.at[batch], pair_recv.at[batch], partner,
        )

    def pair_gather(batch, half):
        part = w16.at[taps(batch), :, pl.ds(pl.multiple_of(128 * half, 128), 128)]
        n = len(BATCHES) + batch
        return remote(part, part, pair_send.at[n], pair_recv.at[n], partner)

    def ring(stage, batch, kw, d, src, dst, axis):
        n = ((stage * len(BATCHES) + batch) * 3 + kw) * 3 + d
        return remote(src, dst, ring_send.at[n], ring_recv.at[n], moved(at, axis, d + 1))

    def order(kw):
        return AXES[kw], AXES[(kw + 1) % 3], AXES[(kw + 2) % 3]

    def tile(p, base=0):
        return (
            pl.ds(pl.multiple_of(base + 16 * (p // 2), 16), 16),
            pl.ds(pl.multiple_of(128 * (p % 2), 128), 128),
        )

    def rows32(p, base=0):
        return pl.ds(pl.multiple_of(base + 32 * p, 32), 32)

    def scatter_one(batch, kw, d):
        first = order(kw)[0]
        to = (at[first] + d + 1) % 4
        return ring(
            0, batch, kw, d, s1.at[kw, taps(batch), rows32(to)], r1.at[kw, d, taps(batch)], first
        )

    def scatter_two(batch, kw, d):
        second = order(kw)[1]
        rows, cols = tile((at[second] + d + 1) % 4)
        return ring(
            1, batch, kw, d, s2.at[kw, taps(batch), rows, cols], r2.at[kw, d, taps(batch)], second
        )

    def sum_three(batch, kw, d):
        part = taps(batch)
        return ring(2, batch, kw, d, s3.at[kw, part], r3.at[kw, d, part], order(kw)[2])

    def gather_two(batch, kw, d, back=0):
        first, second, _ = order(kw)
        rows, cols = tile((at[second] + 4 - back) % 4, 128 * c + 32 * at[first])
        part = w16.at[taps(batch), kw, rows, cols]
        return ring(3, batch, kw, d, part, part, second)

    def gather_one(batch, kw, d, back=0):
        first = order(kw)[0]
        part = w16.at[taps(batch), kw, rows32((at[first] + 4 - back) % 4, 128 * c)]
        return ring(4, batch, kw, d, part, part, first)

    def each_tap(batch):
        first, count = BATCHES[batch]
        return range(first, first + count)

    def start_pair(batch):
        pair_sum(batch).start()

    def start_one(batch):
        pair_sum(batch).wait_recv()
        mine = pl.ds(pl.multiple_of(128 * c, 128), 128)
        for kw in range(3):
            for n in each_tap(batch):
                s1[kw, n] = (w[n, kw, mine] + r0[n, kw]).astype(BF16)
            for d in range(3):
                scatter_one(batch, kw, d).start()

    def start_two(batch):
        for kw in range(3):
            p = at[order(kw)[0]]
            for d in range(3):
                scatter_one(batch, kw, d).wait_recv()
            for n in each_tap(batch):
                total = w[n, kw, rows32(p, 128 * c)] + r0[n, kw, rows32(p)]
                for d in range(3):
                    total = total + r1[kw, d, n].astype(F32)
                s2[kw, n] = total
            for d in range(3):
                scatter_two(batch, kw, d).start()

    def start_three(batch):
        part = taps(batch)
        for kw in range(3):
            rows, cols = tile(at[order(kw)[1]])
            for d in range(3):
                scatter_two(batch, kw, d).wait_recv()
            total = s2[kw, part, rows, cols]
            for d in range(3):
                total = total + r2[kw, d, part]
            s3[kw, part] = total
            for d in range(3):
                sum_three(batch, kw, d).start()

    def start_gather_two(batch):
        part = taps(batch)
        for kw in range(3):
            first, second, _ = order(kw)
            rows, cols = tile(at[second], 128 * c + 32 * at[first])
            for d in range(3):
                sum_three(batch, kw, d).wait_recv()
            total = (s3[kw, part] + r3[kw, 1, part]) + (r3[kw, 0, part] + r3[kw, 2, part])
            w16[part, kw, rows, cols] = total.astype(BF16)
            for d in range(3):
                gather_two(batch, kw, d).start()

    def start_gather_one(batch):
        for kw in range(3):
            for d in range(3):
                gather_two(batch, kw, d, d + 1).wait_recv()
            for d in range(3):
                gather_one(batch, kw, d).start()

    def start_pair_gather(batch):
        for kw in range(3):
            for d in range(3):
                gather_one(batch, kw, d, d + 1).wait_recv()
        pair_gather(batch, c).start()

    def finish(batch):
        pair_gather(batch, 1 - c).wait_recv()

    halos[0].wait_send()
    halos[1].wait_send()
    halos[3].start()
    halos[4].start()
    halos[0].wait_recv()
    halos[1].wait_recv()
    edge_rows((0, 1))
    halos[5].start()
    halos[6].start()
    weight_part(0, (HERE,))
    for t in (0, 1):
        turn(t, 0)
        turn(t, 4)
    weight_part(3, (HERE,))
    weight_part(4, (HERE,))

    halos[2].wait_recv()

    @pl.when(f == 31)
    def _():
        for row in (1, 2, 3):
            clear((4, 5), row)

    for t in (4, 5):
        for row in (1, 2, 3):
            turn(t, row)
    weight_part(1, (HERE, NEXT))
    weight_part(2, (HERE, NEXT))
    start_pair(0)
    loads[2].wait()

    halos[3].wait_recv()
    halos[4].wait_recv()
    edge_rows((2, 3))
    for t in (2, 3):
        turn(t, 0)
        turn(t, 4)
    weight_part(3, (ABOVE_BELOW,), more=True)
    weight_part(4, (ABOVE_BELOW,), more=True)
    start_pair(1)
    start_one(0)
    halos[5].wait_recv()
    halos[6].wait_recv()

    @pl.when(f == 31)
    def _():
        for row in (0, 4):
            clear((4, 5), row)

    for t in (4, 5):
        turn(t, 0)
        turn(t, 4)
    everything = (HERE, ABOVE_BELOW, NEXT)
    weight_part(5, everything)
    weight_part(6, everything)
    start_pair(2)
    start_one(1)
    start_two(0)
    weight_part(7, everything)
    weight_part(8, everything)
    start_pair(3)
    start_one(2)
    start_two(1)
    start_three(0)

    chunks = [(t, h) for t in range(4) for h in range(3)]
    steps = (
        None, (start_one, 3), (start_two, 2), (start_three, 1), (start_gather_two, 0), None,
        (start_two, 3), (start_three, 2), (start_gather_two, 1), (start_gather_one, 0), None,
        (start_three, 3), (start_gather_two, 2), (start_gather_one, 1), (start_pair_gather, 0), None,
        (start_gather_two, 3), (start_gather_one, 2), (start_pair_gather, 1), (finish, 0), None,
        (start_gather_one, 3), (start_pair_gather, 2), (finish, 1), None, (finish, 2),
    )
    for step in steps:
        if step is None:
            input_grad(*chunks.pop(0))
            input_grad(*chunks.pop(0))
        else:
            step[0](step[1])
    start_pair_gather(3)
    finish(3)

    for copy in halos[2:]:
        copy.wait_send()
    for batch in range(len(BATCHES)):
        pair_sum(batch).wait_send()
        pair_gather(batch, c).wait_send()
        for kw in range(3):
            for d in range(3):
                for step in (scatter_one, scatter_two, sum_three, gather_two, gather_one):
                    step(batch, kw, d).wait_send()


def fused(acts, grad_out, kernel):
    flops = 4 * 27 * 256 * 256 * 3072
    dma = pltpu.SemaphoreType.DMA
    return pl.pallas_call(
        body,
        out_shape=(
            pltpu.VMEM(acts.shape, BF16),
            pltpu.VMEM((9, 3, 256, 256), BF16),
        ),
        in_specs=[pl.BlockSpec(memory_space=pl.ANY)] * 3,
        out_specs=(pl.BlockSpec(memory_space=pltpu.VMEM),) * 2,
        scratch_shapes=[
            pltpu.VMEM((4, 3, 256, 256), BF16),
            pltpu.VMEM((6, 5, 256, 256), BF16),
            pltpu.VMEM((6, 5, 256, 256), BF16),
            pltpu.VMEM((3, 3, 3, 256, 256), BF16),
            pltpu.VMEM((4, 3, 3, 256, 256), BF16),
            pltpu.VMEM((4, 3, 256, 256), F32),
            pltpu.VMEM((9, 3, 256, 256), F32),
            pltpu.VMEM((9, 3, 128, 256), F32),
            pltpu.VMEM((3, 9, 128, 256), BF16),
            pltpu.VMEM((3, 3, 9, 32, 256), BF16),
            pltpu.VMEM((3, 9, 32, 256), F32),
            pltpu.VMEM((3, 3, 9, 16, 128), F32),
            pltpu.VMEM((3, 9, 16, 128), F32),
            pltpu.VMEM((3, 3, 9, 16, 128), F32),
            dma((3,)),
            dma((7,)),
            dma((7,)),
            dma((2 * len(BATCHES),)),
            dma((2 * len(BATCHES),)),
            dma((45 * len(BATCHES),)),
            dma((45 * len(BATCHES),)),
        ],
        compiler_params=pltpu.CompilerParams(
            collective_id=0, has_side_effects=True, vmem_limit_bytes=58 * 2**20
        ),
        cost_estimate=pl.CostEstimate(flops=flops, bytes_accessed=16_000_000, transcendentals=0),
        name="conv_grads",
    )(acts, grad_out, kernel)


def write_body(scale, gout, w16, gacts_hbm, wgrad_hbm, wide, sems):
    copies = [pltpu.make_async_copy(gout, gacts_hbm, sems.at[len(TAPS)])]
    copies[0].start()
    for n, (kt, kh) in enumerate(TAPS):
        wide[n] = w16[n].astype(F32) * scale
        copies.append(pltpu.make_async_copy(wide.at[n], wgrad_hbm.at[kt, kh], sems.at[n]))
        copies[-1].start()
    for copy in copies:
        copy.wait()


def on_device(acts, grad_out, kernel):
    cells = 1
    for dim, axis in ((0, "frames"), (1, "rows")):
        cells *= acts.shape[dim] * lax.axis_size(axis)
    cells *= acts.shape[3]
    return pl.pallas_call(
        functools.partial(write_body, 1.0 / math.sqrt(cells)),
        out_shape=(
            jax.ShapeDtypeStruct(acts.shape, BF16),
            jax.ShapeDtypeStruct(kernel.shape, F32),
        ),
        in_specs=[pl.BlockSpec(memory_space=pltpu.VMEM)] * 2,
        out_specs=(pl.BlockSpec(memory_space=pl.ANY),) * 2,
        scratch_shapes=[
            pltpu.VMEM((9, 3, 256, 256), F32),
            pltpu.SemaphoreType.DMA((1 + len(TAPS),)),
        ],
        compiler_params=pltpu.CompilerParams(vmem_limit_bytes=16 * 2**20),
        name="write_out",
    )(*fused(acts, grad_out, kernel))


def solution(mesh):
    placed = (P("frames", "rows", None, None), P("frames", "rows", None, None), P())
    return jax.shard_map(
        on_device,
        mesh=mesh,
        in_specs=placed,
        out_specs=(P("frames", "rows", None, None), P()),
        check_vma=False,
    )
```

time: 334 us -> 67.9 us (0.20); the launches traced: 330 us -> 67.8 us
  matrix products: 118 us -> 0 us
  waiting for transfers between devices: 108 us -> 0 us
  Pallas kernels: 0 us -> 67 us
  local copies, waits for them, and re-layouts: 52.7 us -> 0 us
  starting transfers between devices: 22.8 us -> 0 us
  between operations: 14.9 us -> 0.8 us
  other arithmetic: 13.6 us -> 0 us
    dot_general x54 -> x0, matrix products: 118 us -> none  [the longest x27 98.8 us: on_device(): jnp.einsum('thow,io->thiw', piece, kernel[kt, kh, kw], preferred_element_...]
    psum x1 -> x0, waiting for transfers between devices: 101 us -> none  [on_device(): total = lax.psum(local_sum, ('frames', 'rows'))]
    pallas_call x0 -> x2, Pallas kernels: none -> 67 us  [the longest x1 63.5 us: fused(): pl.pallas_call(body, out_shape=(pltpu.VMEM(acts.shape, BF16), pltpu.VMEM(...]
    slice x5 -> x0, local copies, waits for them, and re-layouts: 32.9 us -> none  [the longest x3 31.8 us: on_device(): act_ext[kt:kt + frames_here, kh:kh + rows_here, :, kw:kw + width_here]]
    ppermute x6 -> x0, starting transfers between devices: 22.8 us -> none  [the longest x2 10.5 us: from_behind(): lax.ppermute(value, axis, [(source, source + steps) for source in range(i...]
    unnamed x67 -> x0, local copies, waits for them, and re-layouts: 19.9 us -> none
    mul x1 -> x0, other arithmetic: 6.92 us -> none  [on_device(): weight_grad = total * (1.0 / math.sqrt(cells))]
    ppermute x6 -> x0, waiting for transfers between devices: 6.86 us -> none  [the longest x2 6.85 us: padded(): lax.ppermute(head, axis, [((i + 1) % count, i) for i in range(ends)])]
  transfers between devices with their start and end apart: 7 -> 0, of which waited for: 3 -> 0; matrix products, arithmetic and copies ran while one was open for 33% -> 0% of each run, Pallas kernels for 0% -> 0%
where the time goes in v2:
time: 67.9 us; the launch traced here: 67.8 us
  Pallas kernels  67 us (99%)
  between operations  0.8 us (1%)
    pallas_call x1, Pallas kernels, fused(): pl.pallas_call(body, out_shape=(pltpu.VMEM(acts.shape, BF16), pltpu.VMEM(...  63.5 us
    pallas_call x1, Pallas kernels, on_device(): pl.pallas_call(functools.partial(write_body, 1.0 / math.sqrt(cells)), out...  3.47 us

profile of v2, /device:TPU:1, one launch (start us, length us, event | category | flops | bytes accessed | tf_op | source)
XLA Modules:
  0.0 67.8 jit_solution(5234701673167870854)
XLA Ops:
  0.6 63.5 %conv_grads.1 = (bf16[4,3,256,256]{3,2,1,0:T(8,128)(2,1)S(1)}, bf16[9,3,256,256]{3,2,1,0:T(8,128)(2,1)S(1)}) custom-call(bf16[4,3,256,256]{3,2,1,0:T(8,128)(2,1)} %acts_hbm.1, bf16[4,3,256,256]{3,2,1,0:T(8,128)(2,1)} %grad_hbm.1, bf16[3,3,3,256,256]{4,3,2,1,0:T(8,128)(2,1)} %kern_hbm.1), custom_call_target="tpu_custom_call" | custom-call | flops 21743271936 | bytes 16000000 | tf_op jit(solution)/shard_map/conv_grads/pallas_call | solution.py:375
  64.2 3.5 %write_out.1 = (bf16[4,3,256,256]{3,2,1,0:T(8,128)(2,1)}, f32[3,3,3,256,256]{4,3,2,1,0:T(8,128)}) custom-call(bf16[4,3,256,256]{3,2,1,0:T(8,128)(2,1)S(1)} %get-tuple-element.4.gout, bf16[9,3,256,256]{3,2,1,0:T(8,128)(2,1)S(1)} %get-tuple-element.5.w16), custom_call_target="tpu_custom_call" | custom-call | tf_op jit(solution)/shard_map/write_out/pallas_call | solution.py:430

commit v3 on v2

--- a/solution.py
+++ b/solution.py
@@ -12,7 +12,9 @@
 BF16, F32 = jnp.bfloat16, jnp.float32
 AXES = "xyz"
 TAPS = ((2, 1), (1, 1), (0, 1), (2, 0), (2, 2), (1, 0), (1, 2), (0, 0), (0, 2))
-BATCHES = ((0, 3), (3, 2), (5, 2), (7, 2))
+BATCHES = ((0, 3), (3, 2), (5, 4))
+FAR_FIRST = (1, 0, 2)
+LAST = len(BATCHES) - 1
 
 
 def place():
@@ -34,7 +36,7 @@
 def body(
     acts_hbm, grad_hbm, kern_hbm, gout, w16,
     acts, g, gt, k, a3, slope, w, r0, s1, r1, s2, r2, s3, r3,
-    local_sem, halo_send, halo_recv, pair_send, pair_recv, ring_send, ring_recv,
+    local_sem, halo_send, halo_recv, pair_send, pair_recv, ring_send, ring_recv, cross_send, cross_recv,
 ):
     at = place()
     c = at["core"]
@@ -54,6 +56,7 @@
     barrier = pltpu.get_barrier_semaphore()
     peers = [partner, (f_prev, r), (f_next, r)]
     peers += [moved(at, axis, d) for axis in AXES for d in (1, 2, 3)]
+    peers += [moved({**at, "core": 1 - c}, axis, d) for axis in AXES for d in (1, 2, 3)]
     for peer in peers:
         pl.semaphore_signal(barrier, inc=1, device_id=peer, device_id_type=MESH)
     pl.semaphore_wait(barrier, len(peers))
@@ -95,7 +98,7 @@
     def turn(t, row):
         gt[t, row] = g[t, row].T
 
-    HERE, ABOVE_BELOW, NEXT = range(3)
+    HERE, EDGE, NEXT, CORNER = range(4)
 
     def weight_part(n, parts, more=False):
         kt, kh = TAPS[n]
@@ -103,7 +106,9 @@
         for t in range(4):
             for h in range(3):
                 frame, row = t + 2 - kt, h + 2 - kh
-                part = NEXT if frame > 3 else HERE if 1 <= row <= 3 else ABOVE_BELOW
+                part = (NEXT if frame > 3 else HERE) if 1 <= row <= 3 else (
+                    CORNER if frame > 3 else EDGE
+                )
                 if part not in parts:
                     continue
                 term = jnp.dot(
@@ -150,15 +155,16 @@
     def taps(batch):
         return pl.ds(*BATCHES[batch])
 
-    def pair_sum(batch):
+    def pair_sum(batch, kw):
+        n = batch * 3 + kw
         return remote(
-            w.at[taps(batch), :, pl.ds(pl.multiple_of(128 * (1 - c), 128), 128)],
-            r0.at[taps(batch)], pair_send.at[batch], pair_recv.at[batch], partner,
+            w.at[taps(batch), kw, pl.ds(pl.multiple_of(128 * (1 - c), 128), 128)],
+            r0.at[taps(batch), kw], pair_send.at[n], pair_recv.at[n], partner,
         )
 
-    def pair_gather(batch, half):
-        part = w16.at[taps(batch), :, pl.ds(pl.multiple_of(128 * half, 128), 128)]
-        n = len(BATCHES) + batch
+    def pair_gather(batch, kw, half):
+        part = w16.at[taps(batch), kw, pl.ds(pl.multiple_of(128 * half, 128), 128)]
+        n = (len(BATCHES) + batch) * 3 + kw
         return remote(part, part, pair_send.at[n], pair_recv.at[n], partner)
 
     def ring(stage, batch, kw, d, src, dst, axis):
@@ -206,20 +212,29 @@
         part = w16.at[taps(batch), kw, rows32((at[first] + 4 - back) % 4, 128 * c)]
         return ring(4, batch, kw, d, part, part, first)
 
+    def gather_cross(batch, kw, d, incoming=False):
+        first = order(kw)[0]
+        half, p = (1 - c, (at[first] + 3 - d) % 4) if incoming else (c, at[first])
+        part = w16.at[taps(batch), kw, rows32(p, 128 * half)]
+        n = kw * 4 + d
+        to = moved({**at, "core": 1 - c}, first, d + 1)
+        return remote(part, part, cross_send.at[n], cross_recv.at[n], to)
+
     def each_tap(batch):
         first, count = BATCHES[batch]
         return range(first, first + count)
 
     def start_pair(batch):
-        pair_sum(batch).start()
+        for kw in range(3):
+            pair_sum(batch, kw).start()
 
     def start_one(batch):
-        pair_sum(batch).wait_recv()
         mine = pl.ds(pl.multiple_of(128 * c, 128), 128)
         for kw in range(3):
+            pair_sum(batch, kw).wait_recv()
             for n in each_tap(batch):
                 s1[kw, n] = (w[n, kw, mine] + r0[n, kw]).astype(BF16)
-            for d in range(3):
+            for d in FAR_FIRST:
                 scatter_one(batch, kw, d).start()
 
     def start_two(batch):
@@ -232,7 +247,7 @@
                 for d in range(3):
                     total = total + r1[kw, d, n].astype(F32)
                 s2[kw, n] = total
-            for d in range(3):
+            for d in FAR_FIRST:
                 scatter_two(batch, kw, d).start()
 
     def start_three(batch):
@@ -245,7 +260,7 @@
             for d in range(3):
                 total = total + r2[kw, d, part]
             s3[kw, part] = total
-            for d in range(3):
+            for d in FAR_FIRST:
                 sum_three(batch, kw, d).start()
 
     def start_gather_two(batch):
@@ -257,24 +272,36 @@
                 sum_three(batch, kw, d).wait_recv()
             total = (s3[kw, part] + r3[kw, 1, part]) + (r3[kw, 0, part] + r3[kw, 2, part])
             w16[part, kw, rows, cols] = total.astype(BF16)
-            for d in range(3):
+            for d in FAR_FIRST:
                 gather_two(batch, kw, d).start()
 
     def start_gather_one(batch):
         for kw in range(3):
             for d in range(3):
                 gather_two(batch, kw, d, d + 1).wait_recv()
-            for d in range(3):
+            for d in FAR_FIRST:
                 gather_one(batch, kw, d).start()
+            if batch == LAST:
+                for d in range(4):
+                    gather_cross(batch, kw, d).start()
 
     def start_pair_gather(batch):
         for kw in range(3):
             for d in range(3):
                 gather_one(batch, kw, d, d + 1).wait_recv()
-        pair_gather(batch, c).start()
+            if batch == LAST:
+                for d in range(4):
+                    gather_cross(batch, kw, d, incoming=True).wait_recv()
+            if batch != LAST:
+                pair_gather(batch, kw, c).start()
 
     def finish(batch):
-        pair_gather(batch, 1 - c).wait_recv()
+        if batch != LAST:
+            for kw in range(3):
+                pair_gather(batch, kw, 1 - c).wait_recv()
+
+    weight_part(0, (HERE,))
+    weight_part(3, (HERE,))
 
     halos[0].wait_send()
     halos[1].wait_send()
@@ -285,12 +312,8 @@
     edge_rows((0, 1))
     halos[5].start()
     halos[6].start()
-    weight_part(0, (HERE,))
-    for t in (0, 1):
-        turn(t, 0)
-        turn(t, 4)
-    weight_part(3, (HERE,))
-    weight_part(4, (HERE,))
+    for n in (4, 1, 2, 5, 6, 7, 8):
+        weight_part(n, (HERE,))
 
     halos[2].wait_recv()
 
@@ -302,21 +325,24 @@
     for t in (4, 5):
         for row in (1, 2, 3):
             turn(t, row)
-    weight_part(1, (HERE, NEXT))
-    weight_part(2, (HERE, NEXT))
+    weight_part(1, (NEXT,), more=True)
+    weight_part(2, (NEXT,), more=True)
     start_pair(0)
-    loads[2].wait()
 
     halos[3].wait_recv()
     halos[4].wait_recv()
     edge_rows((2, 3))
-    for t in (2, 3):
+    for t in range(4):
         turn(t, 0)
         turn(t, 4)
-    weight_part(3, (ABOVE_BELOW,), more=True)
-    weight_part(4, (ABOVE_BELOW,), more=True)
+    weight_part(3, (EDGE,), more=True)
+    weight_part(4, (EDGE,), more=True)
     start_pair(1)
     start_one(0)
+    for n in (5, 6, 7, 8):
+        weight_part(n, (EDGE, NEXT), more=True)
+    start_one(1)
+
     halos[5].wait_recv()
     halos[6].wait_recv()
 
@@ -328,45 +354,42 @@
     for t in (4, 5):
         turn(t, 0)
         turn(t, 4)
-    everything = (HERE, ABOVE_BELOW, NEXT)
-    weight_part(5, everything)
-    weight_part(6, everything)
+    weight_part(5, (CORNER,), more=True)
+    weight_part(6, (CORNER,), more=True)
+    weight_part(7, (CORNER,), more=True)
+    weight_part(8, (CORNER,), more=True)
     start_pair(2)
-    start_one(1)
     start_two(0)
-    weight_part(7, everything)
-    weight_part(8, everything)
-    start_pair(3)
-    start_one(2)
-    start_two(1)
-    start_three(0)
+    loads[2].wait()
 
     chunks = [(t, h) for t in range(4) for h in range(3)]
     steps = (
-        None, (start_one, 3), (start_two, 2), (start_three, 1), (start_gather_two, 0), None,
-        (start_two, 3), (start_three, 2), (start_gather_two, 1), (start_gather_one, 0), None,
-        (start_three, 3), (start_gather_two, 2), (start_gather_one, 1), (start_pair_gather, 0), None,
-        (start_gather_two, 3), (start_gather_one, 2), (start_pair_gather, 1), (finish, 0), None,
-        (start_gather_one, 3), (start_pair_gather, 2), (finish, 1), None, (finish, 2),
+        None, (start_two, 1), (start_one, 2), None, (start_three, 0), None, None,
+        (start_gather_two, 0), (start_three, 1), (start_two, 2), None, None,
+        (start_gather_one, 0), (start_gather_two, 1), (start_three, 2), None, None,
+        (start_pair_gather, 0), (start_gather_one, 1), (start_gather_two, 2), None, None,
+        (start_pair_gather, 1), (start_gather_one, 2), None, None, (finish, 0),
+        (start_pair_gather, 2), (finish, 1), (finish, 2),
     )
     for step in steps:
         if step is None:
             input_grad(*chunks.pop(0))
-            input_grad(*chunks.pop(0))
         else:
             step[0](step[1])
-    start_pair_gather(3)
-    finish(3)
 
     for copy in halos[2:]:
         copy.wait_send()
     for batch in range(len(BATCHES)):
-        pair_sum(batch).wait_send()
-        pair_gather(batch, c).wait_send()
-        for kw in range(3):
+        for kw in range(3):
+            pair_sum(batch, kw).wait_send()
+            if batch != LAST:
+                pair_gather(batch, kw, c).wait_send()
             for d in range(3):
                 for step in (scatter_one, scatter_two, sum_three, gather_two, gather_one):
                     step(batch, kw, d).wait_send()
+    for kw in range(3):
+        for d in range(4):
+            gather_cross(LAST, kw, d).wait_send()
 
 
 def fused(acts, grad_out, kernel):
@@ -398,10 +421,12 @@
             dma((3,)),
             dma((7,)),
             dma((7,)),
-            dma((2 * len(BATCHES),)),
-            dma((2 * len(BATCHES),)),
+            dma((6 * len(BATCHES),)),
+            dma((6 * len(BATCHES),)),
             dma((45 * len(BATCHES),)),
             dma((45 * len(BATCHES),)),
+            dma((12,)),
+            dma((12,)),
         ],
         compiler_params=pltpu.CompilerParams(
             collective_id=0, has_side_effects=True, vmem_limit_bytes=58 * 2**20

time: 67.9 us -> 66.3 us (0.976)
  Pallas kernels: 67 us -> 65.4 us
    pallas_call x1, Pallas kernels: 63.5 us -> 61.9 us  [fused(): pl.pallas_call(body, out_shape=(pltpu.VMEM(acts.shape, BF16), pltpu.VMEM(...]
where the time goes in v3:
time: 66.3 us; the launch traced here: 66.2 us
  Pallas kernels  65.4 us (99%)
  between operations  0.8 us (1%)
    pallas_call x1, Pallas kernels, fused(): pl.pallas_call(body, out_shape=(pltpu.VMEM(acts.shape, BF16), pltpu.VMEM(...  61.9 us
    pallas_call x1, Pallas kernels, on_device(): pl.pallas_call(functools.partial(write_body, 1.0 / math.sqrt(cells)), out...  3.47 us

profile of v3, /device:TPU:1, one launch (start us, length us, event | category | flops | bytes accessed | tf_op | source)
XLA Modules:
  0.0 66.2 jit_solution(18434734477431467315)
XLA Ops:
  0.6 61.9 %conv_grads.1 = (bf16[4,3,256,256]{3,2,1,0:T(8,128)(2,1)S(1)}, bf16[9,3,256,256]{3,2,1,0:T(8,128)(2,1)S(1)}) custom-call(bf16[4,3,256,256]{3,2,1,0:T(8,128)(2,1)} %acts_hbm.1, bf16[4,3,256,256]{3,2,1,0:T(8,128)(2,1)} %grad_hbm.1, bf16[3,3,3,256,256]{4,3,2,1,0:T(8,128)(2,1)} %kern_hbm.1), custom_call_target="tpu_custom_call" | custom-call | flops 21743271936 | bytes 16000000 | tf_op jit(solution)/shard_map/conv_grads/pallas_call | solution.py:398
  62.6 3.5 %write_out.1 = (bf16[4,3,256,256]{3,2,1,0:T(8,128)(2,1)}, f32[3,3,3,256,256]{4,3,2,1,0:T(8,128)}) custom-call(bf16[4,3,256,256]{3,2,1,0:T(8,128)(2,1)S(1)} %get-tuple-element.4.gout, bf16[9,3,256,256]{3,2,1,0:T(8,128)(2,1)S(1)} %get-tuple-element.5.w16), custom_call_target="tpu_custom_call" | custom-call | tf_op jit(solution)/shard_map/write_out/pallas_call | solution.py:455

commit v4 on v3

--- a/solution.py
+++ b/solution.py
@@ -364,12 +364,12 @@
 
     chunks = [(t, h) for t in range(4) for h in range(3)]
     steps = (
-        None, (start_two, 1), (start_one, 2), None, (start_three, 0), None, None,
-        (start_gather_two, 0), (start_three, 1), (start_two, 2), None, None,
-        (start_gather_one, 0), (start_gather_two, 1), (start_three, 2), None, None,
-        (start_pair_gather, 0), (start_gather_one, 1), (start_gather_two, 2), None, None,
-        (start_pair_gather, 1), (start_gather_one, 2), None, None, (finish, 0),
-        (start_pair_gather, 2), (finish, 1), (finish, 2),
+        (start_one, 2), None, (start_two, 1), (start_three, 0), None, None, (start_two, 2),
+        (start_gather_two, 0), (start_three, 1), None, None, (start_three, 2),
+        (start_gather_one, 0), (start_gather_two, 1), None, None, (start_gather_two, 2),
+        (start_pair_gather, 0), (start_gather_one, 1), None, None, (start_gather_one, 2),
+        (start_pair_gather, 1), None, None, None, (start_pair_gather, 2), (finish, 0),
+        (finish, 1), (finish, 2),
     )
     for step in steps:
         if step is None:

time: 66.3 us -> 65.1 us (0.982)
  Pallas kernels: 65.4 us -> 64.2 us
    pallas_call x1, Pallas kernels: 61.9 us -> 60.7 us  [fused(): pl.pallas_call(body, out_shape=(pltpu.VMEM(acts.shape, BF16), pltpu.VMEM(...]
where the time goes in v4:
time: 65.1 us; the launch traced here: 65 us
  Pallas kernels  64.2 us (99%)
  between operations  0.8 us (1%)
    pallas_call x1, Pallas kernels, fused(): pl.pallas_call(body, out_shape=(pltpu.VMEM(acts.shape, BF16), pltpu.VMEM(...  60.7 us
    pallas_call x1, Pallas kernels, on_device(): pl.pallas_call(functools.partial(write_body, 1.0 / math.sqrt(cells)), out...  3.47 us

profile of v4, /device:TPU:1, one launch (start us, length us, event | category | flops | bytes accessed | tf_op | source)
XLA Modules:
  0.0 65.0 jit_solution(10693685192407416476)
XLA Ops:
  0.6 60.7 %conv_grads.1 = (bf16[4,3,256,256]{3,2,1,0:T(8,128)(2,1)S(1)}, bf16[9,3,256,256]{3,2,1,0:T(8,128)(2,1)S(1)}) custom-call(bf16[4,3,256,256]{3,2,1,0:T(8,128)(2,1)} %acts_hbm.1, bf16[4,3,256,256]{3,2,1,0:T(8,128)(2,1)} %grad_hbm.1, bf16[3,3,3,256,256]{4,3,2,1,0:T(8,128)(2,1)} %kern_hbm.1), custom_call_target="tpu_custom_call" | custom-call | flops 21743271936 | bytes 16000000 | tf_op jit(solution)/shard_map/conv_grads/pallas_call | solution.py:398
  61.4 3.5 %write_out.1 = (bf16[4,3,256,256]{3,2,1,0:T(8,128)(2,1)}, f32[3,3,3,256,256]{4,3,2,1,0:T(8,128)}) custom-call(bf16[4,3,256,256]{3,2,1,0:T(8,128)(2,1)S(1)} %get-tuple-element.4.gout, bf16[9,3,256,256]{3,2,1,0:T(8,128)(2,1)S(1)} %get-tuple-element.5.w16), custom_call_target="tpu_custom_call" | custom-call | tf_op jit(solution)/shard_map/write_out/pallas_call | solution.py:455
